TPU v7x, 128 devices: a whole 4x4x4 slice. The times are simulated.
128 devices in a mesh: space: 16 (over z, y), sub: 8 (over x, core).
Axes of the slice: x: 4, y: 4, z: 4, core: 2. Of those that a mesh axis runs over, the one named last changes fastest.
Arguments:
- coefficients: float32 [13, 20, 262144], P(None, None, ('space', 'sub')), may hold values from -6 to 6
- geometry: float32 [3, 3, 262144], P(None, None, ('space', 'sub')), may hold values from -3.5 to 3.5
- face_scale: float32 [4, 262144], P(None, ('space', 'sub')), may hold values from 0.3 to 1.5
- neighbours: int32 [4, 262144], P(None, ('space', 'sub')), may hold values from 0 to 2560, as said below
- stiffness: float32 [3, 20, 20], replicated, may hold values from -1.25 to 1.25
- face_minus: float32 [4, 20, 20], replicated, may hold values from -1.25 to 1.25
- face_plus: float32 [4, 20, 20], replicated, may hold values from -1.25 to 1.25
- jacobians: float32 [3, 13, 13], replicated, may hold values from -1.75 to 1.75
- flux_minus: float32 [13, 13], replicated, may hold values from -1.75 to 1.75
- flux_plus: float32 [13, 13], replicated, may hold values from -1.75 to 1.75
- face_basis: float32 [16, 20], replicated, may hold values from -1.25 to 1.25
- rotation: float32 [8, 13], replicated, may hold values from -1.75 to 1.75
- lift_quantity: float32 [13, 8], replicated, may hold values from -2 to 2
- lift_basis: float32 [20, 16], replicated, may hold values from -1.5 to 1.5
- send_elements: int32 [128, 128, 8], P(('space', 'sub')), may hold values from 0 to 2047, as said below
- send_count: int32 [128, 128], P(('space', 'sub')), may hold values from 0 to 8, as said below
- minus_slot: int32 [32768], P(('space', 'sub')), may hold values from 0 to 1023, as said below
- plus_slot: int32 [32768], P(('space', 'sub')), may hold values from 0 to 1023, as said below
- normal_stress: float32 [16, 32768], P(None, ('space', 'sub')), may hold values from -8 to -2
- shear_stress: float32 [2, 16, 32768], P(None, None, ('space', 'sub')), may hold values from 0.5 to 3
- pore_pressure: float32 [16, 32768], P(None, ('space', 'sub')), may hold values from 0.2 to 1.5
- initial_rate: float32 [16, 32768], P(None, ('space', 'sub')), may hold values from 0.05 to 2
- initial_state: float32 [16, 32768], P(None, ('space', 'sub')), may hold values from 0.45 to 0.7
- direct_effect: float32 [16, 32768], P(None, ('space', 'sub')), may hold values from 0.08 to 0.2
- evolution_effect: float32 [16, 32768], P(None, ('space', 'sub')), may hold values from 0.08 to 0.3
- slip_length: float32 [16, 32768], P(None, ('space', 'sub')), may hold values from 0.2 to 2
Outputs:
- updated: float32 [13, 20, 262144], P(None, None, ('space', 'sub'))
- slip_rate: float32 [16, 32768], P(None, ('space', 'sub'))
- fault_state: float32 [16, 32768], P(None, ('space', 'sub'))
Inputs may be any that keep to these rules, and one draw needn't show every extreme that they name: `neighbours`: values index extended_p; the last face of every element named by a used slot (c < send_count) is the zero column 2560. `send_elements`: element indices within the sending partition; an element may stand in several slots. `send_count`: for every owner some partition fills all 8 slots of its block; the counts toward one owner sum to 512. For owner o, minus_slot and plus_slot of its 256 faces name 512 distinct slots s * 8 + c, exactly the used ones (c < send_count[s, o]). `plus_slot`: see minus_slot.
All inputs are finite; a program needn't handle non-finite values.
Results may differ from a plain program's by a relative error of at most 0.00045.
Values sent between devices are 32-bit elements; how exact they have to be, the bound alone decides.
No kernel may reach another device: no remote copies, remote signals or barrier semaphores. Data moves between devices by JAX's collectives and lax.ppermute only.
A program may use at most 128 MiB of HBM per device.

v0:
```python
import math

import jax
import jax.numpy as jnp
import numpy as np
from jax import lax
from jax.experimental import pallas as pl
from jax.experimental.pallas import tpu as pltpu
from jax.sharding import PartitionSpec as P

QUANT = 13
BASIS = 20
ORDER = 4
FACES = 4
POINTS = 16
TPOINTS = 4
FQUANT = 8
NEWTON = 6
GHOST = 256
COLS = 512
MAIN_COLS = 1024

time_step = 0.5
friction_ref = 0.6
impedance_normal = 2.0
impedance_shear = 1.2
impedance_fluid = 0.8
rate_floor = 0.01
gauss_inner = 0.3399810435848563
gauss_outer = 0.8611363115940526
weight_inner = 0.6521451548625461
weight_outer = 0.3478548451374538

f32 = jnp.float32
bf16 = jnp.bfloat16
AXES = ("space", "sub")
VMEM_LIMIT = 56 * 1024 * 1024

QUADS = 5
PAIRS = 7
ROWS = 280
QUAD_ROWS = 56
PAIR_ROWS = 40


def pair_tiles(p):
    return [PAIRS * k + p for k in range(QUADS)]


GROUPS = tuple([t for p in pairs for t in pair_tiles(p)] for pairs in ((0, 1), (2, 3), (4, 5, 6)))


def time_tables():
    gauss_nodes = [-gauss_outer, -gauss_inner, gauss_inner, gauss_outer]
    gauss_weights = [weight_outer, weight_inner, weight_inner, weight_outer]
    time_points = [time_step * (1.0 + node_value) / 2.0 for node_value in gauss_nodes]
    widths = [time_step * weight_value / 2.0 for weight_value in gauss_weights]
    taylor = [
        [float(np.float32(point_value**power / math.factorial(power))) for power in range(ORDER)]
        for point_value in time_points
    ]
    return taylor, [float(width_value) for width_value in widths]


def block_of(r, width):
    at = (r * (-(-(1 << 20) // width))) >> 20
    return at, r - at * width


def quad_rows(r):
    return r >> 2, r & 3


def pair_rows(r):
    return (r >> 2) & 1, 4 * (r >> 3) + (r & 3)


def group_rows(pairs):
    def get(r):
        p, local = block_of(r, PAIR_ROWS)
        q, b = pair_rows(local)
        beyond = r >= PAIR_ROWS * pairs
        return jnp.where(beyond, -1, 2 * p + q), jnp.where(beyond, -1, b)

    return get


def field_rows(r):
    k, local = block_of(r, QUAD_ROWS)
    return local >> 2, 4 * k + (local & 3)


def ones_where(cond):
    return jnp.where(cond, 1.0, 0.0)


def dot(a, b):
    return lax.dot_general(a, b, (((1,), (0,)), ((), ())), preferred_element_type=f32)


def dot_t(a, b):
    return lax.dot_general(a, b, (((1,), (1,)), ((), ())), preferred_element_type=f32)


def parts(x, count):
    out = []
    for _ in range(count):
        hi = x.astype(bf16)
        out.append(hi.astype(f32))
        x = x - out[-1]
    return out


def stack_parts(mats, count, pitch):
    pieces = []
    for mat in mats:
        pad = jnp.zeros((pitch - mat.shape[0], mat.shape[1]), f32)
        for part in parts(mat, count):
            pieces += [part, pad]
    return jnp.concatenate(pieces, axis=0).astype(bf16)


def block_matrix(data, pitch, count, layout, row_w, row_blocks, col_w, col_blocks, on_q, triple=False):
    size = data.shape[1]
    mats = data.shape[0] // (pitch * count)
    row_parts = 1 if triple else count
    col_parts = 3 if triple else count
    rows = row_parts * row_blocks * row_w
    cols = col_parts * col_blocks * col_w
    r = lax.broadcasted_iota(jnp.int32, (rows, 1), 0)
    c = lax.broadcasted_iota(jnp.int32, (1, cols), 1)
    row_at, row_local = block_of(r, row_w)
    col_at, col_local = block_of(c, col_w)
    row_q, row_b = layout(row_local)
    col_q, col_b = layout(col_local)
    row_i, row_m = (row_q, row_b) if on_q else (row_b, row_q)
    col_i, col_m = (col_q, col_b) if on_q else (col_b, col_q)
    row_part, row_block = block_of(row_at, row_blocks)
    col_part, col_block = block_of(col_at, col_blocks)
    k = lax.broadcasted_iota(jnp.int32, (size, 1), 0)
    right = ones_where(k == col_i).astype(bf16)
    s = lax.broadcasted_iota(jnp.int32, (1, data.shape[0]), 1)
    mask = row_m == col_m
    if triple:
        s_block, s_local = block_of(s, pitch)
        s_mat = s_block >> 1
        left = ones_where((s_local == row_i) & (s_mat == row_block)).astype(bf16)
        t = lax.broadcasted_iota(jnp.int32, (data.shape[0], 1), 0)
        t_part = block_of(t, pitch)[0] & 1
        wide = dot(data, right)
        wide = jnp.where(t_part == (col_part & 1), wide, 0.0).astype(bf16)
        out = dot(left, wide)
    elif col_blocks == 1:
        left = ones_where(s == (row_block * count + row_part) * pitch + row_i).astype(bf16)
        out = dot(dot(left, data).astype(bf16), right)
        mask = mask & (row_part + col_part < count)
    else:
        s_local = block_of(s, pitch * count)[1]
        left = ones_where(s_local == row_part * pitch + row_i).astype(bf16)
        t = lax.broadcasted_iota(jnp.int32, (data.shape[0], 1), 0)
        wide = dot(data, right)
        wide = jnp.where(block_of(t, pitch * count)[0] == col_block, wide, 0.0).astype(bf16)
        out = dot(left, wide)
        mask = mask & (row_part + col_part < count)
    return jnp.where(mask, out, 0.0).astype(bf16)


def prep_body(
    stiff_ref,
    fm_ref,
    fp_ref,
    jac_ref,
    fluxm_ref,
    fluxp_ref,
    basis_ref,
    rot_ref,
    lq_ref,
    lb_ref,
    jq_ref,
    sp_ref,
    ex_ref,
    ju_ref,
    fa_ref,
    fb_ref,
    jp_ref,
    jq3_ref,
    sp3_ref,
    rb_ref,
    lift_ref,
):
    jac = [jac_ref[x] for x in range(3)]
    minus_stiff = [-stiff_ref[d] for d in range(3)]
    jac_data = stack_parts(jac, 2, 16)
    jq_ref[...] = block_matrix(jac_data, 16, 2, quad_rows, 56, 3, 56, 1, True, True)
    jac_data = stack_parts(jac, 3, 16)
    jq3_ref[...] = block_matrix(jac_data, 16, 3, quad_rows, 56, 3, 56, 1, True)
    for count, ref in ((2, sp_ref), (3, sp3_ref)):
        stiff_data = stack_parts(minus_stiff, count, 24)
        ref[...] = block_matrix(stiff_data, 24, count, pair_rows, 40, 1, 40, 3, False)
    last_data = stack_parts(jac + [-fluxm_ref[...]], 2, 16)
    ju_ref[...] = block_matrix(last_data, 16, 2, quad_rows, 56, 1, 56, 4, True)
    plus_data = stack_parts([-fluxp_ref[...]], 2, 16)
    jp_ref[...] = block_matrix(plus_data, 16, 2, quad_rows, 56, 1, 56, 1, True)
    for f in range(4):
        face_data = stack_parts([fp_ref[:, f, :]], 2, 24)
        fa_ref[f] = block_matrix(face_data, 24, 2, group_rows(2), 80, 1, 128, 1, False)
        fb_ref[f] = block_matrix(face_data, 24, 2, group_rows(3), 120, 1, 128, 1, False)
    expand = [stiff_ref[d].T for d in range(3)] + [fm_ref[:, f, :] for f in range(4)]
    expand_data = stack_parts(expand, 2, 24)
    ex_ref[...] = block_matrix(expand_data, 24, 2, pair_rows, 40, 7, 40, 1, False, True)

    def spread(x, right):
        return sum(dot(part.astype(bf16), right) for part in reversed(parts(x, 3)))

    column = lax.broadcasted_iota(jnp.int32, (1, 3 * ROWS), 1)
    column_part, column = block_of(column, ROWS)
    column_q, column_b = field_rows(column)
    q_id = lax.broadcasted_iota(jnp.int32, (QUANT, 1), 0)
    b_id = lax.broadcasted_iota(jnp.int32, (BASIS, 1), 0)
    rot = spread(rot_ref[...], ones_where(q_id == column_q).astype(bf16))
    bas = spread(basis_ref[...], ones_where(b_id == column_b).astype(bf16))
    full = jnp.concatenate([rot[i : i + 1, :] * bas for i in range(8)], axis=0)
    rows = [jnp.where(column_part < 3 - h, part, 0.0) for h, part in enumerate(parts(full, 3))]
    rb_ref[...] = jnp.concatenate(rows, axis=0).astype(bf16)
    lane = lax.broadcasted_iota(jnp.int32, (1, 256), 1)
    i_id = lax.broadcasted_iota(jnp.int32, (FQUANT, 1), 0)
    k_id = lax.broadcasted_iota(jnp.int32, (POINTS, 1), 0)
    lq = spread(lq_ref[...].T, ones_where(i_id == ((lane >> 4) & 7)).astype(bf16))
    lb = spread(lb_ref[...].T, ones_where(k_id == (lane & 15)).astype(bf16))
    pieces = []
    upper = lax.broadcasted_iota(jnp.int32, (8, 256), 0) < 4
    for k in range(QUADS):
        quad = lb[4 * k : 4 * k + 4, :]
        quad = jnp.concatenate([quad, quad], axis=0)
        for p in range(PAIRS):
            first = lq[2 * p : 2 * p + 1, :]
            second = lq[2 * p + 1 : 2 * p + 2, :] if p < 6 else jnp.zeros_like(first)
            pieces.append(jnp.where(upper, first, second) * quad)
    hi, lo = parts(jnp.concatenate(pieces, axis=0), 2)
    lo = jnp.where(lane < 128, lo, 0.0)
    lift_ref[...] = jnp.concatenate([hi, lo], axis=0).astype(bf16)


PREP_SHAPES = (
    (168, 168),
    (80, 240),
    (280, 120),
    (112, 448),
    (4, 160, 256),
    (4, 240, 256),
    (112, 112),
    (504, 168),
    (120, 360),
    (384, 3 * ROWS),
    (2 * ROWS, 256),
)


def params(**kw):
    return pltpu.CompilerParams(vmem_limit_bytes=VMEM_LIMIT, **kw)


def prep(*matrices):
    return pl.pallas_call(
        prep_body,
        out_shape=[jax.ShapeDtypeStruct(s, bf16) for s in PREP_SHAPES],
        compiler_params=params(),
        name="prep",
    )(*matrices)


def pick(x, tiles):
    return [x[8 * t : 8 * t + 8, :] for t in tiles]


def fold(out, count):
    size = out.shape[0] // count
    total = out[(count - 1) * size :]
    for h in reversed(range(count - 1)):
        total = out[h * size : (h + 1) * size] + total
    return total


def part_product(matrix, blocks, count):
    right = jnp.concatenate([b for part in blocks for b in part], axis=0)
    return fold(dot(matrix, right.astype(bf16)), count)


def quad(x, k):
    return x[QUAD_ROWS * k : QUAD_ROWS * (k + 1)]


def derivative(field, geo, jq, sp, count):
    pieces = parts(field, count)
    blocks = [[], [], []]
    for k in range(QUADS):
        if count == 2:
            hi, lo = quad(pieces[0], k), quad(pieces[1], k)
            out = dot(jq, jnp.concatenate([hi, hi, lo], axis=0).astype(bf16))
        else:
            out = part_product(jq, [[quad(x, k)] for x in pieces], count)
        for d in range(3):
            blocks[d].append(
                geo[3 * d] * quad(out, 0) + geo[3 * d + 1] * quad(out, 1) + geo[3 * d + 2] * quad(out, 2)
            )
    directed = [parts(jnp.concatenate(block, axis=0), count) for block in blocks]
    tiles = [None] * (PAIRS * QUADS)
    for p in range(PAIRS):
        chosen = pair_tiles(p)
        right = []
        for h in range(count):
            right.append([t for d in range(3) for t in pick(directed[d][h], chosen)])
        out = part_product(sp, right, count)
        for k, t in enumerate(chosen):
            tiles[t] = out[8 * k : 8 * k + 8, :]
    return jnp.concatenate(tiles, axis=0)


def load_field(ref):
    tiles = []
    for k in range(QUADS):
        for p in range(PAIRS):
            low = ref[2 * p, 4 * k : 4 * k + 4, :]
            high = ref[2 * p + 1, 4 * k : 4 * k + 4, :] if p < 6 else jnp.zeros_like(low)
            tiles.append(jnp.concatenate([low, high], axis=0))
    return jnp.concatenate(tiles, axis=0)


def copy_rows(sources, table_ref, picked_ref):
    for base in range(0, len(sources), 32):
        got = [
            table_ref[pl.ds(pl.multiple_of(row * 8, 8), 8), :] for row in sources[base : base + 32]
        ]
        for k, value in enumerate(got):
            picked_ref[8 * (base + k) : 8 * (base + k) + 8, :] = value


def send_body(index_ref, coef_ref, geo_ref, out_ref, table_ref, picked_ref):
    elems = coef_ref.shape[2]
    slots = picked_ref.shape[0] // 8
    for c in range(elems // 128):
        cols = pl.ds(128 * c, 128)
        field = load_field(coef_ref.at[:, :, cols])
        geo = [geo_ref[d, x : x + 1, cols] for d in range(3) for x in range(3)]
        geo = jnp.concatenate(geo + [jnp.zeros((384 - ROWS - 9, 128), f32)], axis=0)
        stacked = jnp.concatenate([field, geo], axis=0)
        for j in range(3):
            table_ref[pl.ds(128 * 8 * c + j, 128, stride=8), :] = stacked[128 * j : 128 * (j + 1)].T

    copy_rows(
        [index_ref[s % 8, s // 8] for s in range(slots)], table_ref, picked_ref
    )
    for j in range(3):
        out_ref[:, :, 128 * j : 128 * (j + 1)] = picked_ref[pl.ds(j, slots, stride=8), :].reshape(
            slots // 8, 8, 128
        )


def send(index, coefficients, geometry):
    elems = coefficients.shape[2]
    slots = index.shape[0] * index.shape[1]
    return pl.pallas_call(
        send_body,
        out_shape=jax.ShapeDtypeStruct((slots // 8, 8, 384), f32),
        in_specs=[
            pl.BlockSpec(memory_space=pltpu.SMEM),
            pl.BlockSpec(memory_space=pltpu.VMEM),
            pl.BlockSpec(memory_space=pltpu.VMEM),
        ],
        out_specs=pl.BlockSpec(memory_space=pltpu.VMEM),
        scratch_shapes=[pltpu.VMEM((elems * 8, 128), f32), pltpu.VMEM((slots * 8, 128), f32)],
        compiler_params=params(),
        name="send",
    )(index, coefficients, geometry)


STEP_WEIGHTS = [time_step ** (power + 1) / math.factorial(power + 1) for power in range(ORDER)]


def main_body(
    coef_ref,
    geo_ref,
    scale_ref,
    jq_ref,
    sp_ref,
    ex_ref,
    ju_ref,
    integ_ref,
    part_ref,
    first_ref,
    last_ref,
):
    step = pl.program_id(0)
    field = load_field(coef_ref)
    geo = [geo_ref[d, x : x + 1, :] for d in range(3) for x in range(3)]
    integ_ref[...] = STEP_WEIGHTS[0] * field
    current = field
    for power in range(1, ORDER):
        current = derivative(current, geo, jq_ref[...], sp_ref[...], 2)
        integ_ref[...] += STEP_WEIGHTS[power] * current
    integrated = integ_ref[...]

    @pl.when(step == 0)
    def _():
        first_ref[...] = integrated[:, :GHOST]

    @pl.when(step == pl.num_programs(0) - 1)
    def _():
        last_ref[...] = integrated[:, integrated.shape[1] - GHOST :]

    hi, lo = parts(integrated, 2)
    pieces = [[None] * (PAIRS * QUADS) for _ in range(4)]
    scale = [scale_ref[f : f + 1, :] for f in range(4)]
    for p in range(PAIRS):
        chosen = pair_tiles(p)
        right = pick(hi, chosen) + pick(hi, chosen) + pick(lo, chosen)
        out = dot(ex_ref[...], jnp.concatenate(right, axis=0).astype(bf16))
        blocks = [out[PAIR_ROWS * k : PAIR_ROWS * (k + 1)] for k in range(7)]
        results = [
            geo[x] * blocks[0] + geo[3 + x] * blocks[1] + geo[6 + x] * blocks[2] for x in range(3)
        ]
        results.append(
            scale[0] * blocks[3] + scale[1] * blocks[4] + scale[2] * blocks[5] + scale[3] * blocks[6]
        )
        for m in range(4):
            for k, t in enumerate(chosen):
                pieces[m][t] = results[m][8 * k : 8 * k + 8]
    pairs = [parts(jnp.concatenate(tiles, axis=0), 2) for tiles in pieces]
    for k in range(QUADS):
        out = part_product(ju_ref[...], [[quad(pair[h], k) for pair in pairs] for h in range(2)], 2)
        rows = slice(QUAD_ROWS * k, QUAD_ROWS * (k + 1))
        part_ref[rows, :] = field[rows] + out


def whole(array):
    shape = array.shape
    return pl.BlockSpec(shape, lambda *_: (0,) * len(shape))


def main(coefficients, geometry, face_scale, mats):
    elems = coefficients.shape[2]
    block = pl.BlockSpec((ROWS, MAIN_COLS), lambda i: (0, i))
    fixed = pl.BlockSpec((ROWS, GHOST), lambda i: (0, 0))
    field = jax.ShapeDtypeStruct((ROWS, elems), f32)
    rim = jax.ShapeDtypeStruct((ROWS, GHOST), f32)
    return pl.pallas_call(
        main_body,
        grid=(elems // MAIN_COLS,),
        out_shape=[field, field, rim, rim],
        in_specs=[
            pl.BlockSpec((QUANT, BASIS, MAIN_COLS), lambda i: (0, 0, i)),
            pl.BlockSpec((3, 3, MAIN_COLS), lambda i: (0, 0, i)),
            pl.BlockSpec((FACES, MAIN_COLS), lambda i: (0, i)),
        ]
        + [whole(m) for m in mats],
        out_specs=[block, block, fixed, fixed],
        compiler_params=params(),
        name="main",
    )(coefficients, geometry, face_scale, *mats)


def inverse_sinh(value):
    magnitude = jnp.abs(value)
    result = jnp.log(magnitude + jnp.sqrt(magnitude * magnitude + 1.0))
    return jnp.where(value < 0.0, -result, result)


def friction(minus, plus, ns, ss, pp, rate, state, direct, evolution, slip, widths):
    damping = 0.5 * impedance_shear
    slip_rate = rate
    state_now = state
    back = [[0.0] * 8, [0.0] * 8]
    for j in range(TPOINTS):
        m = [minus(i, j) for i in range(8)]
        n = [plus(i, j) for i in range(8)]
        normal_mid = 0.5 * (m[0] + n[0]) + 0.5 * impedance_normal * (n[3] - m[3])
        shear_one = 0.5 * (m[1] + n[1]) + 0.5 * impedance_shear * (n[4] - m[4])
        shear_two = 0.5 * (m[2] + n[2]) + 0.5 * impedance_shear * (n[5] - m[5])
        fluid_mid = 0.5 * (m[6] + n[6]) + 0.5 * impedance_fluid * (n[7] - m[7])
        effective = jnp.maximum(-(ns + normal_mid + pp + fluid_mid), 0.0)
        total_one = ss[0] + shear_one
        total_two = ss[1] + shear_two
        locked = jnp.sqrt(total_one * total_one + total_two * total_two + 1.0)
        scaled = 0.5 * jnp.exp(state_now / direct)
        floor_term = 4.0 * jnp.exp(-2.0 * state_now / direct)
        strength_rate = effective * direct
        for sweep in range(NEWTON):
            residual = strength_rate * inverse_sinh(scaled * slip_rate) + damping * slip_rate - locked
            slope = strength_rate / jnp.sqrt(floor_term + slip_rate * slip_rate) + damping
            slip_rate = slip_rate - residual / slope
        steady = friction_ref - (evolution - direct) * 0.5 * jnp.log(
            slip_rate * slip_rate + rate_floor
        )
        state_now = steady + (state_now - steady) * jnp.exp(-jnp.abs(slip_rate) * widths[j] / slip)
        strength = locked - damping * slip_rate
        traction_one = strength * total_one / locked - ss[0]
        traction_two = strength * total_two / locked - ss[1]
        h = widths[j]
        for side, t, sign in ((0, m, 1.0), (1, n, -1.0)):
            d0 = normal_mid - t[0]
            d1 = traction_one - t[1]
            d2 = traction_two - t[2]
            d6 = fluid_mid - t[6]
            changes = [
                d0,
                d1,
                d2,
                d0 * (sign / impedance_normal),
                d1 * (sign / impedance_shear),
                d2 * (sign / impedance_shear),
                d6,
                d6 * (sign / impedance_fluid),
            ]
            for i in range(8):
                back[side][i] = back[side][i] + h * changes[i]
    return slip_rate, state_now, back[0], back[1]


def fault_body(
    minus_ref,
    plus_ref,
    arr_ref,
    jq_ref,
    sp_ref,
    rb_ref,
    ns_ref,
    ss_ref,
    pp_ref,
    rate_ref,
    state_ref,
    direct_ref,
    evol_ref,
    slip_ref,
    ret_ref,
    rate_out,
    state_out,
    table_ref,
    picked_ref,
    trace_ref,
    rows_ref,
):
    slots = table_ref.shape[0] // 8
    sides = picked_ref.shape[0] // 8
    faces = sides // 2
    for j in range(3):
        table_ref[pl.ds(j, slots, stride=8), :] = arr_ref[:, :, 128 * j : 128 * (j + 1)].reshape(
            slots, 128
        )

    slot_ids = [ref[s] for ref in (minus_ref, plus_ref) for s in range(faces)]
    copy_rows(slot_ids, table_ref, picked_ref)
    taylor, widths = time_tables()
    columns = []
    for c in range(sides // 128):
        columns.append(
            jnp.concatenate(
                [picked_ref[pl.ds(1024 * c + j, 128, stride=8), :].T for j in range(3)], axis=0
            )
        )
    stacked = jnp.concatenate(columns, axis=1)
    current = stacked[:ROWS]
    geo = [stacked[ROWS + k : ROWS + k + 1] for k in range(9)]
    for m in range(ORDER):
        if m > 0:
            current = derivative(current, geo, jq_ref[...], sp_ref[...], 3)
        trace_ref[m] = part_product(rb_ref[...], [[x] for x in parts(current, 3)], 3)

    def trace_of(side):
        def get(i, j):
            cols = slice(side * faces, (side + 1) * faces)
            value = trace_ref[0, 16 * i : 16 * i + 16, cols] * taylor[j][0]
            for m in range(1, ORDER):
                value = value + taylor[j][m] * trace_ref[m, 16 * i : 16 * i + 16, cols]
            return value

        return get

    slip_rate, state_now, back_minus, back_plus = friction(
        trace_of(0),
        trace_of(1),
        ns_ref[...],
        (ss_ref[0], ss_ref[1]),
        pp_ref[...],
        rate_ref[...],
        state_ref[...],
        direct_ref[...],
        evol_ref[...],
        slip_ref[...],
        widths,
    )
    rate_out[...] = slip_rate
    state_out[...] = state_now
    for side, back in ((0, back_minus), (1, back_plus)):
        stacked = jnp.concatenate(back, axis=0)
        for c in range(faces // 128):
            rows_ref[pl.ds(side * faces + 128 * c, 128), :] = stacked[:, 128 * c : 128 * (c + 1)].T
    ret_ref[...] = jnp.zeros_like(ret_ref)

    for s in range(sides):
        ret_ref[pl.ds(slot_ids[s], 1), :] = rows_ref[s : s + 1, :]


def fault(minus_slot, plus_slot, arrived, mats, fields):
    slots = arrived.shape[0] * arrived.shape[1]
    faces = minus_slot.shape[0]
    sides = 2 * faces
    point = jax.ShapeDtypeStruct((POINTS, faces), f32)
    vmem = pl.BlockSpec(memory_space=pltpu.VMEM)
    return pl.pallas_call(
        fault_body,
        out_shape=[jax.ShapeDtypeStruct((slots, 128), f32), point, point],
        in_specs=[pl.BlockSpec(memory_space=pltpu.SMEM)] * 2 + [vmem] * (1 + len(mats) + len(fields)),
        out_specs=[vmem] * 3,
        scratch_shapes=[
            pltpu.VMEM((slots * 8, 128), f32),
            pltpu.VMEM((sides * 8, 128), f32),
            pltpu.VMEM((ORDER, 128, sides), f32),
            pltpu.VMEM((sides, 128), f32),
        ],
        compiler_params=params(),
        name="fault",
    )(minus_slot, plus_slot, arrived, *mats, *fields)


def beside_body(
    index_ref,
    integ_ref,
    low_ref,
    high_ref,
    part_ref,
    scale_ref,
    fa_ref,
    fb_ref,
    jp_ref,
    out_ref,
    table_ref,
    picked_ref,
):
    step = pl.program_id(0)
    elems = integ_ref.shape[1]

    @pl.when(step == 0)
    def _():
        for source, first, count in (
            (low_ref, 0, GHOST),
            (integ_ref, GHOST, elems),
            (high_ref, GHOST + elems, GHOST),
        ):
            for c in range(count // 128):
                field = source[:, 128 * c : 128 * (c + 1)]
                for j, tiles in enumerate(GROUPS):
                    rows = pick(field, tiles)
                    pad = 128 - 8 * len(tiles)
                    stacked = jnp.concatenate(rows + [jnp.zeros((pad, 128), f32)], axis=0)
                    table_ref[pl.ds(8 * (first + 128 * c) + j, 128, stride=8), :] = stacked.T
        table_ref[pl.ds(8 * (elems + 2 * GHOST), 8), :] = jnp.zeros((8, 128), f32)

    scale = [scale_ref[f : f + 1, :] for f in range(4)]
    total = [None] * (PAIRS * QUADS)
    for f in range(FACES):
        copy_rows([index_ref[f, s] for s in range(COLS)], table_ref, picked_ref)
        for j, tiles in enumerate(GROUPS):
            hi, lo = parts(picked_ref[pl.ds(j, COLS, stride=8), :], 2)
            right = jnp.concatenate([hi, lo], axis=1).astype(bf16)
            out = dot_t(fb_ref[f] if j == 2 else fa_ref[f], right)
            half = out.shape[0] // 2
            out = scale[f] * (out[:half] + out[half:])
            for k, t in enumerate(tiles):
                value = out[8 * k : 8 * k + 8]
                total[t] = value if total[t] is None else total[t] + value
    hi, lo = parts(jnp.concatenate(total, axis=0), 2)
    for k in range(QUADS):
        out = part_product(jp_ref[...], [[quad(hi, k)], [quad(lo, k)]], 2)
        rows = slice(QUAD_ROWS * k, QUAD_ROWS * (k + 1))
        out_ref[rows, :] = part_ref[rows, :] + out


def beside(neighbours, integrated, low, high, partial, face_scale, mats):
    elems = integrated.shape[1]
    block = pl.BlockSpec((ROWS, COLS), lambda i: (0, i))
    return pl.pallas_call(
        beside_body,
        grid=(elems // COLS,),
        out_shape=jax.ShapeDtypeStruct((ROWS, elems), f32),
        in_specs=[
            pl.BlockSpec((FACES, COLS), lambda i: (0, i), memory_space=pltpu.SMEM),
            whole(integrated),
            whole(low),
            whole(high),
            block,
            pl.BlockSpec((FACES, COLS), lambda i: (0, i)),
        ]
        + [whole(m) for m in mats],
        out_specs=block,
        scratch_shapes=[
            pltpu.VMEM(((elems + 2 * GHOST + 8) * 8, 128), f32),
            pltpu.VMEM((COLS * 8, 128), f32),
        ],
        compiler_params=params(),
        name="beside",
    )(neighbours, integrated, low, high, partial, face_scale, *mats)


def lift_body(elem_ref, back_ref, part_ref, scale_ref, lift_ref, out_ref):
    step = pl.program_id(0)
    cols = out_ref.shape[2]
    capacity, owners = elem_ref.shape
    values, chosen = [], []
    ids = lax.broadcasted_iota(jnp.int32, (cols, owners), 0) + step * cols
    for c in range(capacity):
        hi, lo = parts(back_ref[pl.ds(c, owners, stride=capacity), :], 2)
        values.append(jnp.concatenate([hi, lo], axis=1).astype(bf16))
        chosen.append(ones_where(ids == elem_ref[c : c + 1, :]).astype(bf16))
    summed = dot(jnp.concatenate(chosen, axis=1), jnp.concatenate(values, axis=0))
    hi, lo = parts(summed[:, :128] + summed[:, 128:], 2)
    out = dot_t(lift_ref[...], jnp.concatenate([hi, lo], axis=1).astype(bf16))
    out = part_ref[...] + scale_ref[FACES - 1 : FACES, :] * (out[:ROWS] + out[ROWS:])
    for q in range(13):
        for k in range(QUADS):
            at = QUAD_ROWS * k + 4 * q
            out_ref[q, 4 * k : 4 * k + 4, :] = out[at : at + 4]


def lift(elem_row, back, partial, face_scale, matrix):
    elems = partial.shape[1]
    cols = 512
    return pl.pallas_call(
        lift_body,
        grid=(elems // cols,),
        out_shape=jax.ShapeDtypeStruct((QUANT, BASIS, elems), f32),
        in_specs=[
            whole(elem_row),
            whole(back),
            pl.BlockSpec((ROWS, cols), lambda i: (0, i)),
            pl.BlockSpec((FACES, cols), lambda i: (0, i)),
            whole(matrix),
        ],
        out_specs=pl.BlockSpec((QUANT, BASIS, cols), lambda i: (0, 0, i)),
        compiler_params=params(),
        name="lift",
    )(elem_row, back, partial, face_scale, matrix)


def shards(
    coefficients,
    geometry,
    face_scale,
    neighbours,
    stiffness,
    face_minus,
    face_plus,
    jacobians,
    flux_minus,
    flux_plus,
    face_basis,
    rotation,
    lift_quantity,
    lift_basis,
    send_elements,
    send_count,
    minus_slot,
    plus_slot,
    normal_stress,
    shear_stress,
    pore_pressure,
    initial_rate,
    initial_state,
    direct_effect,
    evolution_effect,
    slip_length,
):
    part_count = send_elements.shape[1]
    capacity = send_elements.shape[2]
    slot_total = part_count * capacity
    slot_elements = jnp.transpose(send_elements[0])
    outgoing = send(slot_elements, coefficients, geometry)
    arrived = lax.all_to_all(outgoing, AXES, split_axis=0, concat_axis=0, tiled=True)
    mats = prep(
        stiffness,
        jnp.transpose(face_minus, (1, 0, 2)),
        jnp.transpose(face_plus, (1, 0, 2)),
        jacobians,
        flux_minus,
        flux_plus,
        face_basis,
        rotation,
        lift_quantity.T,
        lift_basis.T,
    )
    jq, sp, ex, ju, fa, fb, jp, jq3, sp3, rb, lift_matrix = mats
    integrated, partial, first, last = main(
        coefficients, geometry, face_scale, (jq, sp, ex, ju)
    )
    arrived, first, last = lax.optimization_barrier((arrived, first, last))
    count = part_count
    forward = [(i, i + 1) for i in range(count - 1)]
    backward = [(target, source) for source, target in forward]
    low = lax.ppermute(last, AXES, forward)
    high = lax.ppermute(first, AXES, backward)
    returned, slip_rate, fault_state = fault(
        minus_slot,
        plus_slot,
        arrived,
        (jq3, sp3, rb),
        (
            normal_stress,
            shear_stress,
            pore_pressure,
            initial_rate,
            initial_state,
            direct_effect,
            evolution_effect,
            slip_length,
        ),
    )
    returned, low, high = lax.optimization_barrier((returned, low, high))
    back = lax.all_to_all(
        returned.reshape(part_count, capacity, 128), AXES, split_axis=0, concat_axis=0, tiled=True
    )
    partial = beside(neighbours, integrated, low, high, partial, face_scale, (fa, fb, jp))
    updated = lift(
        slot_elements,
        back.reshape(slot_total, 128),
        partial,
        face_scale,
        lift_matrix,
    )
    return (updated, slip_rate, fault_state)


def solution(mesh):
    cols = P(None, AXES)
    in_specs = (
        P(None, None, AXES),
        P(None, None, AXES),
        cols,
        cols,
        *(P() for _ in range(10)),
        P(AXES, None, None),
        P(AXES, None),
        P(AXES),
        P(AXES),
        cols,
        P(None, None, AXES),
        *(cols for _ in range(6)),
    )
    out_specs = (P(None, None, AXES), cols, cols)
    return jax.shard_map(shards, mesh=mesh, in_specs=in_specs, out_specs=out_specs, check_vma=False)
```

profile of v0, /device:TPU:1, one launch (start us, length us, event | category | flops | bytes accessed | tf_op | source)
XLA Modules:
  0.0 94.9 jit_solution(6617686550515542815)
XLA Ops:
  0.6 5.1 %send.1 = f32[128,8,384]{2,1,0:T(8,128)} custom-call(s32[8,128]{1,0:T(8,128)} %bitcast.13, f32[13,20,2048]{2,1,0:T(8,128)} %coef_ref.3, f32[3,3,2048]{2,1,0:T(4,128)} %geo_ref.3), custom_call_target="tpu_custom_call" | custom-call | tf_op jit(solution)/shard_map/send/pallas_call | solution.py:362
  5.7 11.5 %all-to-all-start = ((f32[128,8,384]{2,1,0:T(8,128)}), f32[128,8,384]{2,1,0:T(8,128)S(1)}, u32[]{:S(2)}, u32[]{:S(2)}) async-start(f32[128,8,384]{2,1,0:T(8,128)} %send.1), calls=%async_computation | async-start | bytes 3145728 | tf_op jit(solution)/shard_map/all_to_all | solution.py:777
  17.2 4.0 %prep.1 = (bf16[168,168]{1,0:T(8,128)(2,1)}, bf16[80,240]{1,0:T(8,128)(2,1)}, bf16[280,120]{1,0:T(8,128)(2,1)}, bf16[112,448]{1,0:T(8,128)(2,1)}, bf16[4,160,256...) custom-call(f32[3,20,20]{2,1,0:T(8,128)} %stiff_ref.1, ...), custom_call_target="tpu_custom_call" | custom-call | tf_op jit(solution)/shard_map/prep/pallas_call | solution.py:264
  21.3 20.2 %main.1 = (f32[280,2048]{1,0:T(8,128)}, f32[280,2048]{1,0:T(8,128)}, f32[280,256]{1,0:T(8,128)}, f32[280,256]{1,0:T(8,128)}) custom-call(f32[13,20,2048]{2,1,0:T(8,128)} %coef_ref.3, f32[3,3,2048]{2,1,0:T(4,128)} %geo_ref.3, f32[4,2048]{1,0:T(4,128)} %scale_ref.5, bf16[168,168]{1,0:T(8,128)(2,1)} %get-tuple-element.27.jq_ref, ...), custom_call_target="tpu_custom_call" | custom-call | tf_op jit(solution)/shard_map/main/pallas_call | solution.py:446
  41.5 0.7 all-to-all-done.arr_ref
  42.1 0.0 copy-start
  42.1 3.0 %collective-permute-start = (f32[280,256]{1,0:T(8,128)}, f32[280,256]{1,0:T(8,128)S(1)}, u32[]{:S(2)}, u32[]{:S(2)}) collective-permute-start(f32[280,256]{1,0:T(8,128)} %get-tuple-element.38), channel_id=1, source_target_pairs={{0,1},{1,2},{2,3},{3,4},{4,5},{5,6},{6,7},{7,8},{8,9},{9,10},{10,1... | collective-permute-start | bytes 860168 | tf_op jit(solution)/shard_map/ppermute | solution.py:798
  45.1 2.1 %collective-permute-start.1 = (f32[280,256]{1,0:T(8,128)}, f32[280,256]{1,0:T(8,128)S(1)}, u32[]{:S(2)}, u32[]{:S(2)}) collective-permute-start(f32[280,256]{1,0:T(8,128)} %get-tuple-element.39), channel_id=1, source_target_pairs={{1,0},{2,1},{3,2},{4,3},{5,4},{6,5},{7,6},{8,7},{9,8},{10,9},{11,1... | collective-permute-start | bytes 860168 | tf_op jit(solution)/shard_map/ppermute | solution.py:799
  47.3 0.0 copy-done
  47.3 13.1 %fault.1 = (f32[1024,128]{1,0:T(8,128)}, f32[16,256]{1,0:T(8,128)}, f32[16,256]{1,0:T(8,128)}) custom-call(s32[256]{0:T(256)} %minus_ref.1, s32[256]{0:T(256)} %plus_ref.1, f32[128,8,384]{2,1,0:T(8,128)} %copy-done, bf16[504,168]{1,0:T(8,128)(2,1)} %get-tuple-element.34.jq_ref, bf16[120,360]{1,0:T(8,128)(2,1)} %get-tuple-element.35.sp_ref, ...), custom_call_target="tpu_custom_call" | custom-call | tf_op jit(solution)/shard_map/fault/pallas_call | solution.py:609
  60.4 0.0 collective-permute-done.low_ref
  60.5 0.0 copy-start.2
  60.5 0.0 collective-permute-done.1.high_ref
  60.5 0.0 copy-start.3
  60.5 9.8 %all-to-all-start.1 = ((f32[128,8,128]{2,1,0:T(8,128)}), f32[128,8,128]{2,1,0:T(8,128)S(1)}, u32[]{:S(2)}, u32[]{:S(2)}) async-start(f32[128,8,128]{2,1,0:T(8,128)} %bitcast.10), calls=%async_computation.1 | async-start | bytes 1048576 | tf_op jit(solution)/shard_map/all_to_all | solution.py:817
  70.3 0.0 copy-done.2
  70.3 0.0 copy-done.3
  70.3 17.1 %beside.1.part_ref = f32[280,2048]{1,0:T(8,128)} custom-call(s32[4,2048]{1,0:T(4,128)} %index_ref.1, f32[280,2048]{1,0:T(8,128)} %get-tuple-element.41.integ_ref, f32[280,256]{1,0:T(8,128)} %copy-done.2, f32[280,256]{1,0:T(8,128)} %copy-done.3, f32[280,2048]{1,0:T(8,128)} %get-tuple-element.44.part_ref, f32[4,2048]{1,0:T(4,128)} %scale_ref.5, ...), custom_call_target="tpu_custom_call" | custom-call | tf_op jit(solution)/shard_map/beside/pallas_call | solution.py:681
  87.4 0.0 all-to-all-done.1
  87.4 0.0 copy-start.1
  87.4 0.8 copy-done.1
  88.2 6.7 %lift.1 = f32[13,20,2048]{2,1,0:T(8,128)} custom-call(s32[8,128]{1,0:T(8,128)} %bitcast.14, f32[1024,128]{1,0:T(8,128)} %bitcast.9, f32[280,2048]{1,0:T(8,128)} %beside.1.part_ref, f32[4,2048]{1,0:T(4,128)} %scale_ref.5, bf16[560,256]{1,0:T(8,128)(2,1)} %get-tuple-element.48.lift_ref), custom_call_target="tpu_custom_call" | custom-call | tf_op jit(solution)/shard_map/lift/pallas_call | solution.py:727
Async XLA Ops:
  5.7 36.4 %all-to-all-start = ((f32[128,8,384]{2,1,0:T(8,128)}), f32[128,8,384]{2,1,0:T(8,128)S(1)}, u32[]{:S(2)}, u32[]{:S(2)}) async-start(f32[128,8,384]{2,1,0:T(8,128)} %send.1), calls=%async_computation | async-start | bytes 3145728 | tf_op jit(solution)/shard_map/all_to_all | solution.py:777
  42.1 5.2 %copy-start = (f32[128,8,384]{2,1,0:T(8,128)}, f32[128,8,384]{2,1,0:T(8,128)S(1)}, u32[]{:S(2)}) copy-start(f32[128,8,384]{2,1,0:T(8,128)S(1)} %all-to-all-done.arr_ref) | copy-start | bytes 4718596
  42.1 18.3 %collective-permute-start = (f32[280,256]{1,0:T(8,128)}, f32[280,256]{1,0:T(8,128)S(1)}, u32[]{:S(2)}, u32[]{:S(2)}) collective-permute-start(f32[280,256]{1,0:T(8,128)} %get-tuple-element.38), channel_id=1, source_target_pairs={{0,1},{1,2},{2,3},{3,4},{4,5},{5,6},{6,7},{7,8},{8,9},{9,10},{10,1... | collective-permute-start | bytes 860168 | tf_op jit(solution)/shard_map/ppermute | solution.py:798
  45.1 15.3 %collective-permute-start.1 = (f32[280,256]{1,0:T(8,128)}, f32[280,256]{1,0:T(8,128)S(1)}, u32[]{:S(2)}, u32[]{:S(2)}) collective-permute-start(f32[280,256]{1,0:T(8,128)} %get-tuple-element.39), channel_id=1, source_target_pairs={{1,0},{2,1},{3,2},{4,3},{5,4},{6,5},{7,6},{8,7},{9,8},{10,9},{11,1... | collective-permute-start | bytes 860168 | tf_op jit(solution)/shard_map/ppermute | solution.py:799
  60.5 9.8 %copy-start.2 = (f32[280,256]{1,0:T(8,128)}, f32[280,256]{1,0:T(8,128)S(1)}, u32[]{:S(2)}) copy-start(f32[280,256]{1,0:T(8,128)S(1)} %collective-permute-done.low_ref) | copy-start | bytes 860164
  60.5 9.8 %copy-start.3 = (f32[280,256]{1,0:T(8,128)}, f32[280,256]{1,0:T(8,128)S(1)}, u32[]{:S(2)}) copy-start(f32[280,256]{1,0:T(8,128)S(1)} %collective-permute-done.1.high_ref) | copy-start | bytes 860164
  60.5 26.9 %all-to-all-start.1 = ((f32[128,8,128]{2,1,0:T(8,128)}), f32[128,8,128]{2,1,0:T(8,128)S(1)}, u32[]{:S(2)}, u32[]{:S(2)}) async-start(f32[128,8,128]{2,1,0:T(8,128)} %bitcast.10), calls=%async_computation.1 | async-start | bytes 1048576 | tf_op jit(solution)/shard_map/all_to_all | solution.py:817
  87.4 0.8 copy-start.1
where the time goes:
time: 95.5 us; the launch traced here: 94.9 us
  Pallas kernels  66.3 us (69%)
  starting transfers between devices  26.4 us (28%)
    pallas_call x1, Pallas kernels, main(): pl.pallas_call(main_body, grid=(elems // MAIN_COLS,), out_shape=[field, f...  20.2 us
    pallas_call x1, Pallas kernels, beside(): pl.pallas_call(beside_body, grid=(elems // COLS,), out_shape=jax.ShapeDty...  17.1 us
    pallas_call x1, Pallas kernels, fault(): pl.pallas_call(fault_body, out_shape=[jax.ShapeDtypeStruct((slots, 128),...  13.1 us
    all_to_all x1, starting transfers between devices, shards(): lax.all_to_all(outgoing, AXES, split_axis=0, concat_axis=0, tiled=True)  11.5 us
    all_to_all x1, starting transfers between devices, shards(): lax.all_to_all(returned.reshape(part_count, capacity, 128), AXES, split_a...  9.78 us
    pallas_call x1, Pallas kernels, lift(): pl.pallas_call(lift_body, grid=(elems // cols,), out_shape=jax.ShapeDtype...  6.7 us
    pallas_call x1, Pallas kernels, send(): pl.pallas_call(send_body, out_shape=jax.ShapeDtypeStruct((slots // 8, 8,...  5.08 us
    pallas_call x1, Pallas kernels, prep(): pl.pallas_call(prep_body, out_shape=[jax.ShapeDtypeStruct(s, bf16) for s...  4.03 us
  transfers between devices with their start and end apart: 4, of which 1 were waited for; matrix products, arithmetic and copies ran while one was open for 0% of the time, Pallas kernels for 57%

commit v1 on v0

--- a/solution.py
+++ b/solution.py
@@ -329,7 +329,7 @@
 def copy_rows(sources, table_ref, picked_ref):
     for base in range(0, len(sources), 32):
         got = [
-            table_ref[pl.ds(pl.multiple_of(row * 8, 8), 8), :] for row in sources[base : base + 32]
+            table_ref[pl.ds(pl.multiple_of(row, 8), 8), :] for row in sources[base : base + 32]
         ]
         for k, value in enumerate(got):
             picked_ref[8 * (base + k) : 8 * (base + k) + 8, :] = value
@@ -348,7 +348,7 @@
             table_ref[pl.ds(128 * 8 * c + j, 128, stride=8), :] = stacked[128 * j : 128 * (j + 1)].T
 
     copy_rows(
-        [index_ref[s % 8, s // 8] for s in range(slots)], table_ref, picked_ref
+        [index_ref[s % 8, s // 8] * 8 for s in range(slots)], table_ref, picked_ref
     )
     for j in range(3):
         out_ref[:, :, 128 * j : 128 * (j + 1)] = picked_ref[pl.ds(j, slots, stride=8), :].reshape(
@@ -381,6 +381,7 @@
     coef_ref,
     geo_ref,
     scale_ref,
+    beside_ref,
     jq_ref,
     sp_ref,
     ex_ref,
@@ -389,8 +390,10 @@
     part_ref,
     first_ref,
     last_ref,
+    row_ref,
 ):
     step = pl.program_id(0)
+    row_ref[...] = beside_ref[...] * 8
     field = load_field(coef_ref)
     geo = [geo_ref[d, x : x + 1, :] for d in range(3) for x in range(3)]
     integ_ref[...] = STEP_WEIGHTS[0] * field
@@ -437,7 +440,7 @@
     return pl.BlockSpec(shape, lambda *_: (0,) * len(shape))
 
 
-def main(coefficients, geometry, face_scale, mats):
+def main(coefficients, geometry, face_scale, neighbours, mats):
     elems = coefficients.shape[2]
     block = pl.BlockSpec((ROWS, MAIN_COLS), lambda i: (0, i))
     fixed = pl.BlockSpec((ROWS, GHOST), lambda i: (0, 0))
@@ -446,17 +449,24 @@
     return pl.pallas_call(
         main_body,
         grid=(elems // MAIN_COLS,),
-        out_shape=[field, field, rim, rim],
+        out_shape=[field, field, rim, rim, jax.ShapeDtypeStruct(neighbours.shape, jnp.int32)],
         in_specs=[
             pl.BlockSpec((QUANT, BASIS, MAIN_COLS), lambda i: (0, 0, i)),
             pl.BlockSpec((3, 3, MAIN_COLS), lambda i: (0, 0, i)),
             pl.BlockSpec((FACES, MAIN_COLS), lambda i: (0, i)),
+            pl.BlockSpec((FACES, MAIN_COLS), lambda i: (0, i)),
         ]
         + [whole(m) for m in mats],
-        out_specs=[block, block, fixed, fixed],
+        out_specs=[
+            block,
+            block,
+            fixed,
+            fixed,
+            pl.BlockSpec((FACES, MAIN_COLS), lambda i: (0, i)),
+        ],
         compiler_params=params(),
         name="main",
-    )(coefficients, geometry, face_scale, *mats)
+    )(coefficients, geometry, face_scale, neighbours, *mats)
 
 
 def inverse_sinh(value):
@@ -548,7 +558,7 @@
         )
 
     slot_ids = [ref[s] for ref in (minus_ref, plus_ref) for s in range(faces)]
-    copy_rows(slot_ids, table_ref, picked_ref)
+    copy_rows([slot * 8 for slot in slot_ids], table_ref, picked_ref)
     taylor, widths = time_tables()
     columns = []
     for c in range(sides // 128):
@@ -701,17 +711,24 @@
     )(neighbours, integrated, low, high, partial, face_scale, *mats)
 
 
-def lift_body(elem_ref, back_ref, part_ref, scale_ref, lift_ref, out_ref):
+def lift_body(elem_ref, back_ref, part_ref, scale_ref, lift_ref, out_ref, values_ref):
     step = pl.program_id(0)
     cols = out_ref.shape[2]
     capacity, owners = elem_ref.shape
-    values, chosen = [], []
+    chosen = []
+
+    @pl.when(step == 0)
+    def _():
+        for c in range(capacity):
+            hi, lo = parts(back_ref[pl.ds(c, owners, stride=capacity), :], 2)
+            values_ref[owners * c : owners * (c + 1), :] = jnp.concatenate([hi, lo], axis=1).astype(
+                bf16
+            )
+
     ids = lax.broadcasted_iota(jnp.int32, (cols, owners), 0) + step * cols
     for c in range(capacity):
-        hi, lo = parts(back_ref[pl.ds(c, owners, stride=capacity), :], 2)
-        values.append(jnp.concatenate([hi, lo], axis=1).astype(bf16))
         chosen.append(ones_where(ids == elem_ref[c : c + 1, :]).astype(bf16))
-    summed = dot(jnp.concatenate(chosen, axis=1), jnp.concatenate(values, axis=0))
+    summed = dot(jnp.concatenate(chosen, axis=1), values_ref[...])
     hi, lo = parts(summed[:, :128] + summed[:, 128:], 2)
     out = dot_t(lift_ref[...], jnp.concatenate([hi, lo], axis=1).astype(bf16))
     out = part_ref[...] + scale_ref[FACES - 1 : FACES, :] * (out[:ROWS] + out[ROWS:])
@@ -723,7 +740,7 @@
 
 def lift(elem_row, back, partial, face_scale, matrix):
     elems = partial.shape[1]
-    cols = 512
+    cols = 1024
     return pl.pallas_call(
         lift_body,
         grid=(elems // cols,),
@@ -736,6 +753,7 @@
             whole(matrix),
         ],
         out_specs=pl.BlockSpec((QUANT, BASIS, cols), lambda i: (0, 0, i)),
+        scratch_shapes=[pltpu.VMEM(back.shape[:1] + (256,), bf16)],
         compiler_params=params(),
         name="lift",
     )(elem_row, back, partial, face_scale, matrix)
@@ -788,8 +806,8 @@
         lift_basis.T,
     )
     jq, sp, ex, ju, fa, fb, jp, jq3, sp3, rb, lift_matrix = mats
-    integrated, partial, first, last = main(
-        coefficients, geometry, face_scale, (jq, sp, ex, ju)
+    integrated, partial, first, last, rows = main(
+        coefficients, geometry, face_scale, neighbours, (jq, sp, ex, ju)
     )
     arrived, first, last = lax.optimization_barrier((arrived, first, last))
     count = part_count
@@ -817,7 +835,7 @@
     back = lax.all_to_all(
         returned.reshape(part_count, capacity, 128), AXES, split_axis=0, concat_axis=0, tiled=True
     )
-    partial = beside(neighbours, integrated, low, high, partial, face_scale, (fa, fb, jp))
+    partial = beside(rows, integrated, low, high, partial, face_scale, (fa, fb, jp))
     updated = lift(
         slot_elements,
         back.reshape(slot_total, 128),

time: 95.5 us -> 93.7 us (0.981)
  Pallas kernels: 66.3 us -> 64.6 us
    pallas_call x1, Pallas kernels: 17.1 us -> 15.8 us  [beside(): pl.pallas_call(beside_body, grid=(elems // COLS,), out_shape=jax.ShapeDty...]
where the time goes in v1:
time: 93.7 us; the launch traced here: 93.2 us
  Pallas kernels  64.6 us (69%)
  starting transfers between devices  26.5 us (28%)
    pallas_call x1, Pallas kernels, main(): pl.pallas_call(main_body, grid=(elems // MAIN_COLS,), out_shape=[field, f...  20.3 us
    pallas_call x1, Pallas kernels, beside(): pl.pallas_call(beside_body, grid=(elems // COLS,), out_shape=jax.ShapeDty...  15.8 us
    pallas_call x1, Pallas kernels, fault(): pl.pallas_call(fault_body, out_shape=[jax.ShapeDtypeStruct((slots, 128),...  13.2 us
    all_to_all x1, starting transfers between devices, shards(): lax.all_to_all(outgoing, AXES, split_axis=0, concat_axis=0, tiled=True)  11.5 us
    all_to_all x1, starting transfers between devices, shards(): lax.all_to_all(returned.reshape(part_count, capacity, 128), AXES, split_a...  9.81 us
    pallas_call x1, Pallas kernels, lift(): pl.pallas_call(lift_body, grid=(elems // cols,), out_shape=jax.ShapeDtype...  6.16 us
    pallas_call x1, Pallas kernels, send(): pl.pallas_call(send_body, out_shape=jax.ShapeDtypeStruct((slots // 8, 8,...  5.11 us
    pallas_call x1, Pallas kernels, prep(): pl.pallas_call(prep_body, out_shape=[jax.ShapeDtypeStruct(s, bf16) for s...  4.03 us
  transfers between devices with their start and end apart: 4, of which 1 were waited for; matrix products, arithmetic and copies ran while one was open for 0% of the time, Pallas kernels for 57%

profile of v1, /device:TPU:1, one launch (start us, length us, event | category | flops | bytes accessed | tf_op | source)
XLA Modules:
  0.0 93.2 jit_solution(4127991412403727873)
XLA Ops:
  0.6 5.1 %send.1 = f32[128,8,384]{2,1,0:T(8,128)} custom-call(s32[8,128]{1,0:T(8,128)} %bitcast.13, f32[13,20,2048]{2,1,0:T(8,128)} %coef_ref.3, f32[3,3,2048]{2,1,0:T(4,128)} %geo_ref.3), custom_call_target="tpu_custom_call" | custom-call | tf_op jit(solution)/shard_map/send/pallas_call | solution.py:362
  5.7 11.5 %all-to-all-start = ((f32[128,8,384]{2,1,0:T(8,128)}), f32[128,8,384]{2,1,0:T(8,128)S(1)}, u32[]{:S(2)}, u32[]{:S(2)}) async-start(f32[128,8,384]{2,1,0:T(8,128)} %send.1), calls=%async_computation | async-start | bytes 3145728 | tf_op jit(solution)/shard_map/all_to_all | solution.py:795
  17.3 4.0 %prep.1 = (bf16[168,168]{1,0:T(8,128)(2,1)}, bf16[80,240]{1,0:T(8,128)(2,1)}, bf16[280,120]{1,0:T(8,128)(2,1)}, bf16[112,448]{1,0:T(8,128)(2,1)}, bf16[4,160,256...) custom-call(f32[3,20,20]{2,1,0:T(8,128)} %stiff_ref.1, ...), custom_call_target="tpu_custom_call" | custom-call | tf_op jit(solution)/shard_map/prep/pallas_call | solution.py:264
  21.3 20.3 %main.1 = (f32[280,2048]{1,0:T(8,128)}, f32[280,2048]{1,0:T(8,128)}, f32[280,256]{1,0:T(8,128)}, f32[280,256]{1,0:T(8,128)}, s32[4,2048]{1,0:T(4,128)}) custom-call(f32[13,20,2048]{2,1,0:T(8,128)} %coef_ref.3, f32[3,3,2048]{2,1,0:T(4,128)} %geo_ref.3, f32[4,2048]{1,0:T(4,128)} %scale_ref.5, s32[4,2048]{1,0:T(4,128)} %beside_ref.1, ...), custom_call_target="tpu_custom_call" | custom-call | tf_op jit(solution)/shard_map/main/pallas_call | solution.py:449
  41.5 0.6 all-to-all-done.arr_ref
  42.2 0.0 copy-start
  42.2 3.0 %collective-permute-start = (f32[280,256]{1,0:T(8,128)}, f32[280,256]{1,0:T(8,128)S(1)}, u32[]{:S(2)}, u32[]{:S(2)}) collective-permute-start(f32[280,256]{1,0:T(8,128)} %get-tuple-element.39), channel_id=1, source_target_pairs={{0,1},{1,2},{2,3},{3,4},{4,5},{5,6},{6,7},{7,8},{8,9},{9,10},{10,1... | collective-permute-start | bytes 860168 | tf_op jit(solution)/shard_map/ppermute | solution.py:816
  45.2 2.1 %collective-permute-start.1 = (f32[280,256]{1,0:T(8,128)}, f32[280,256]{1,0:T(8,128)S(1)}, u32[]{:S(2)}, u32[]{:S(2)}) collective-permute-start(f32[280,256]{1,0:T(8,128)} %get-tuple-element.40), channel_id=1, source_target_pairs={{1,0},{2,1},{3,2},{4,3},{5,4},{6,5},{7,6},{8,7},{9,8},{10,9},{11,1... | collective-permute-start | bytes 860168 | tf_op jit(solution)/shard_map/ppermute | solution.py:817
  47.3 0.0 copy-done
  47.3 13.2 %fault.1 = (f32[1024,128]{1,0:T(8,128)}, f32[16,256]{1,0:T(8,128)}, f32[16,256]{1,0:T(8,128)}) custom-call(s32[256]{0:T(256)} %minus_ref.1, s32[256]{0:T(256)} %plus_ref.1, f32[128,8,384]{2,1,0:T(8,128)} %copy-done, bf16[504,168]{1,0:T(8,128)(2,1)} %get-tuple-element.35.jq_ref, bf16[120,360]{1,0:T(8,128)(2,1)} %get-tuple-element.36.sp_ref, ...), custom_call_target="tpu_custom_call" | custom-call | tf_op jit(solution)/shard_map/fault/pallas_call | solution.py:619
  60.5 0.0 collective-permute-done.low_ref
  60.5 0.0 copy-start.2
  60.5 0.0 collective-permute-done.1.high_ref
  60.5 0.0 copy-start.3
  60.6 9.8 %all-to-all-start.1 = ((f32[128,8,128]{2,1,0:T(8,128)}), f32[128,8,128]{2,1,0:T(8,128)S(1)}, u32[]{:S(2)}, u32[]{:S(2)}) async-start(f32[128,8,128]{2,1,0:T(8,128)} %bitcast.10), calls=%async_computation.1 | async-start | bytes 1048576 | tf_op jit(solution)/shard_map/all_to_all | solution.py:835
  70.4 0.0 copy-done.2
  70.4 0.0 copy-done.3
  70.4 15.8 %beside.1.part_ref = f32[280,2048]{1,0:T(8,128)} custom-call(s32[4,2048]{1,0:T(4,128)} %get-tuple-element.42.index_ref, f32[280,2048]{1,0:T(8,128)} %get-tuple-element.43.integ_ref, f32[280,256]{1,0:T(8,128)} %copy-done.2, f32[280,256]{1,0:T(8,128)} %copy-done.3, f32[280,2048]{1,0:T(8,128)} %get-tuple-element.46.part_ref, f32[4,2048]{1,0:T(4,128)} %scale_ref.5, ...), custom_call_target="tpu_custom_call" | custom-call | tf_op jit(solution)/shard_map/beside/pallas_call | solution.py:691
  86.2 0.0 all-to-all-done.1
  86.2 0.0 copy-start.1
  86.2 0.8 copy-done.1
  87.0 6.2 %lift.1 = f32[13,20,2048]{2,1,0:T(8,128)} custom-call(s32[8,128]{1,0:T(8,128)} %bitcast.14, f32[1024,128]{1,0:T(8,128)} %bitcast.9, f32[280,2048]{1,0:T(8,128)} %beside.1.part_ref, f32[4,2048]{1,0:T(4,128)} %scale_ref.5, bf16[560,256]{1,0:T(8,128)(2,1)} %get-tuple-element.50.lift_ref), custom_call_target="tpu_custom_call" | custom-call | tf_op jit(solution)/shard_map/lift/pallas_call | solution.py:744
Async XLA Ops:
  5.7 36.4 %all-to-all-start = ((f32[128,8,384]{2,1,0:T(8,128)}), f32[128,8,384]{2,1,0:T(8,128)S(1)}, u32[]{:S(2)}, u32[]{:S(2)}) async-start(f32[128,8,384]{2,1,0:T(8,128)} %send.1), calls=%async_computation | async-start | bytes 3145728 | tf_op jit(solution)/shard_map/all_to_all | solution.py:795
  42.2 5.2 %copy-start = (f32[128,8,384]{2,1,0:T(8,128)}, f32[128,8,384]{2,1,0:T(8,128)S(1)}, u32[]{:S(2)}) copy-start(f32[128,8,384]{2,1,0:T(8,128)S(1)} %all-to-all-done.arr_ref) | copy-start | bytes 4718596
  42.2 18.3 %collective-permute-start = (f32[280,256]{1,0:T(8,128)}, f32[280,256]{1,0:T(8,128)S(1)}, u32[]{:S(2)}, u32[]{:S(2)}) collective-permute-start(f32[280,256]{1,0:T(8,128)} %get-tuple-element.39), channel_id=1, source_target_pairs={{0,1},{1,2},{2,3},{3,4},{4,5},{5,6},{6,7},{7,8},{8,9},{9,10},{10,1... | collective-permute-start | bytes 860168 | tf_op jit(solution)/shard_map/ppermute | solution.py:816
  45.2 15.4 %collective-permute-start.1 = (f32[280,256]{1,0:T(8,128)}, f32[280,256]{1,0:T(8,128)S(1)}, u32[]{:S(2)}, u32[]{:S(2)}) collective-permute-start(f32[280,256]{1,0:T(8,128)} %get-tuple-element.40), channel_id=1, source_target_pairs={{1,0},{2,1},{3,2},{4,3},{5,4},{6,5},{7,6},{8,7},{9,8},{10,9},{11,1... | collective-permute-start | bytes 860168 | tf_op jit(solution)/shard_map/ppermute | solution.py:817
  60.5 9.9 %copy-start.2 = (f32[280,256]{1,0:T(8,128)}, f32[280,256]{1,0:T(8,128)S(1)}, u32[]{:S(2)}) copy-start(f32[280,256]{1,0:T(8,128)S(1)} %collective-permute-done.low_ref) | copy-start | bytes 860164
  60.5 9.8 %copy-start.3 = (f32[280,256]{1,0:T(8,128)}, f32[280,256]{1,0:T(8,128)S(1)}, u32[]{:S(2)}) copy-start(f32[280,256]{1,0:T(8,128)S(1)} %collective-permute-done.1.high_ref) | copy-start | bytes 860164
  60.6 25.7 %all-to-all-start.1 = ((f32[128,8,128]{2,1,0:T(8,128)}), f32[128,8,128]{2,1,0:T(8,128)S(1)}, u32[]{:S(2)}, u32[]{:S(2)}) async-start(f32[128,8,128]{2,1,0:T(8,128)} %bitcast.10), calls=%async_computation.1 | async-start | bytes 1048576 | tf_op jit(solution)/shard_map/all_to_all | solution.py:835
  86.2 0.8 copy-start.1

commit v2 on v1

--- a/solution.py
+++ b/solution.py
@@ -17,7 +17,7 @@
 FQUANT = 8
 NEWTON = 6
 GHOST = 256
-COLS = 512
+COLS = 1024
 MAIN_COLS = 1024
 
 time_step = 0.5
@@ -120,23 +120,26 @@
     return jnp.concatenate(pieces, axis=0).astype(bf16)
 
 
-def block_matrix(data, pitch, count, layout, row_w, row_blocks, col_w, col_blocks, on_q, triple=False):
+def block_matrix(
+    data, pitch, count, layout, row_w, row_blocks, col_w, col_blocks, on_q, triple=False, col_pitch=0
+):
     size = data.shape[1]
     mats = data.shape[0] // (pitch * count)
     row_parts = 1 if triple else count
     col_parts = 3 if triple else count
     rows = row_parts * row_blocks * row_w
-    cols = col_parts * col_blocks * col_w
+    col_pitch = col_pitch or col_blocks * col_w
+    cols = col_parts * col_pitch
     r = lax.broadcasted_iota(jnp.int32, (rows, 1), 0)
     c = lax.broadcasted_iota(jnp.int32, (1, cols), 1)
     row_at, row_local = block_of(r, row_w)
-    col_at, col_local = block_of(c, col_w)
+    col_part, within = block_of(c, col_pitch)
+    col_block, col_local = block_of(within, col_w)
     row_q, row_b = layout(row_local)
     col_q, col_b = layout(col_local)
     row_i, row_m = (row_q, row_b) if on_q else (row_b, row_q)
     col_i, col_m = (col_q, col_b) if on_q else (col_b, col_q)
     row_part, row_block = block_of(row_at, row_blocks)
-    col_part, col_block = block_of(col_at, col_blocks)
     k = lax.broadcasted_iota(jnp.int32, (size, 1), 0)
     right = ones_where(k == col_i).astype(bf16)
     s = lax.broadcasted_iota(jnp.int32, (1, data.shape[0]), 1)
@@ -196,7 +199,9 @@
     jq3_ref[...] = block_matrix(jac_data, 16, 3, quad_rows, 56, 3, 56, 1, True)
     for count, ref in ((2, sp_ref), (3, sp3_ref)):
         stiff_data = stack_parts(minus_stiff, count, 24)
-        ref[...] = block_matrix(stiff_data, 24, count, pair_rows, 40, 1, 40, 3, False)
+        ref[...] = block_matrix(
+            stiff_data, 24, count, pair_rows, 40, 1, 40, 3, False, col_pitch=128
+        )
     last_data = stack_parts(jac + [-fluxm_ref[...]], 2, 16)
     ju_ref[...] = block_matrix(last_data, 16, 2, quad_rows, 56, 1, 56, 4, True)
     plus_data = stack_parts([-fluxp_ref[...]], 2, 16)
@@ -243,14 +248,14 @@
 
 PREP_SHAPES = (
     (168, 168),
-    (80, 240),
+    (80, 256),
     (280, 120),
     (112, 448),
     (4, 160, 256),
     (4, 240, 256),
     (112, 112),
     (504, 168),
-    (120, 360),
+    (120, 384),
     (384, 3 * ROWS),
     (2 * ROWS, 256),
 )
@@ -271,6 +276,16 @@
 
 def pick(x, tiles):
     return [x[8 * t : 8 * t + 8, :] for t in tiles]
+
+
+def stacked_parts(blocks, count):
+    x = jnp.concatenate(blocks, axis=0)
+    out = []
+    for h in range(count):
+        out.append(x.astype(bf16))
+        if h < count - 1:
+            x = x - out[-1].astype(f32)
+    return jnp.concatenate(out, axis=0)
 
 
 def fold(out, count):
@@ -303,14 +318,13 @@
             blocks[d].append(
                 geo[3 * d] * quad(out, 0) + geo[3 * d + 1] * quad(out, 1) + geo[3 * d + 2] * quad(out, 2)
             )
-    directed = [parts(jnp.concatenate(block, axis=0), count) for block in blocks]
+    directed = [jnp.concatenate(block, axis=0) for block in blocks]
+    pad = [jnp.zeros((8, field.shape[1]), f32)]
     tiles = [None] * (PAIRS * QUADS)
     for p in range(PAIRS):
         chosen = pair_tiles(p)
-        right = []
-        for h in range(count):
-            right.append([t for d in range(3) for t in pick(directed[d][h], chosen)])
-        out = part_product(sp, right, count)
+        right = stacked_parts([t for d in range(3) for t in pick(directed[d], chosen)] + pad, count)
+        out = fold(dot(sp, right), count)
         for k, t in enumerate(chosen):
             tiles[t] = out[8 * k : 8 * k + 8, :]
     return jnp.concatenate(tiles, axis=0)
@@ -428,9 +442,9 @@
         for m in range(4):
             for k, t in enumerate(chosen):
                 pieces[m][t] = results[m][8 * k : 8 * k + 8]
-    pairs = [parts(jnp.concatenate(tiles, axis=0), 2) for tiles in pieces]
+    joined = [jnp.concatenate(tiles, axis=0) for tiles in pieces]
     for k in range(QUADS):
-        out = part_product(ju_ref[...], [[quad(pair[h], k) for pair in pairs] for h in range(2)], 2)
+        out = fold(dot(ju_ref[...], stacked_parts([quad(x, k) for x in joined], 2)), 2)
         rows = slice(QUAD_ROWS * k, QUAD_ROWS * (k + 1))
         part_ref[rows, :] = field[rows] + out
 

time: 93.7 us -> 92 us (0.982)
  Pallas kernels: 64.6 us -> 62.9 us
  waiting for transfers between devices: 0.63 us -> 1.84 us
  starting transfers between devices: 26.5 us -> 25.3 us
    all_to_all x1, waiting for transfers between devices: 0.62 us -> 1.83 us  [shards(): lax.all_to_all(outgoing, AXES, split_axis=0, concat_axis=0, tiled=True)]
    pallas_call x1, Pallas kernels: 20.3 us -> 19 us  [main(): pl.pallas_call(main_body, grid=(elems // MAIN_COLS,), out_shape=[field, f...]
    all_to_all x1, starting transfers between devices: 9.81 us -> 8.61 us  [shards(): lax.all_to_all(returned.reshape(part_count, capacity, 128), AXES, split_a...]
  transfers between devices with their start and end apart: 4 -> 4, of which waited for: 1 -> 1; matrix products, arithmetic and copies ran while one was open for 0% -> 0% of each run, Pallas kernels for 57% -> 56%
where the time goes in v2:
time: 92 us; the launch traced here: 91.5 us
  Pallas kernels  62.9 us (68%)
  starting transfers between devices  25.3 us (28%)
  waiting for transfers between devices  1.84 us (2%)
    pallas_call x1, Pallas kernels, main(): pl.pallas_call(main_body, grid=(elems // MAIN_COLS,), out_shape=[field, f...  19 us
    pallas_call x1, Pallas kernels, beside(): pl.pallas_call(beside_body, grid=(elems // COLS,), out_shape=jax.ShapeDty...  15.5 us
    pallas_call x1, Pallas kernels, fault(): pl.pallas_call(fault_body, out_shape=[jax.ShapeDtypeStruct((slots, 128),...  13.1 us
    all_to_all x1, starting transfers between devices, shards(): lax.all_to_all(outgoing, AXES, split_axis=0, concat_axis=0, tiled=True)  11.5 us
    all_to_all x1, starting transfers between devices, shards(): lax.all_to_all(returned.reshape(part_count, capacity, 128), AXES, split_a...  8.61 us
    pallas_call x1, Pallas kernels, lift(): pl.pallas_call(lift_body, grid=(elems // cols,), out_shape=jax.ShapeDtype...  6.16 us
    pallas_call x1, Pallas kernels, send(): pl.pallas_call(send_body, out_shape=jax.ShapeDtypeStruct((slots // 8, 8,...  5.11 us
    pallas_call x1, Pallas kernels, prep(): pl.pallas_call(prep_body, out_shape=[jax.ShapeDtypeStruct(s, bf16) for s...  4.03 us
  transfers between devices with their start and end apart: 4, of which 1 were waited for; matrix products, arithmetic and copies ran while one was open for 0% of the time, Pallas kernels for 56%

profile of v2, /device:TPU:1, one launch (start us, length us, event | category | flops | bytes accessed | tf_op | source)
XLA Modules:
  0.0 91.5 jit_solution(1219421869809506506)
XLA Ops:
  0.6 5.1 %send.1 = f32[128,8,384]{2,1,0:T(8,128)} custom-call(s32[8,128]{1,0:T(8,128)} %bitcast.13, f32[13,20,2048]{2,1,0:T(8,128)} %coef_ref.3, f32[3,3,2048]{2,1,0:T(4,128)} %geo_ref.3), custom_call_target="tpu_custom_call" | custom-call | tf_op jit(solution)/shard_map/send/pallas_call | solution.py:376
  5.7 11.5 %all-to-all-start = ((f32[128,8,384]{2,1,0:T(8,128)}), f32[128,8,384]{2,1,0:T(8,128)S(1)}, u32[]{:S(2)}, u32[]{:S(2)}) async-start(f32[128,8,384]{2,1,0:T(8,128)} %send.1), calls=%async_computation | async-start | bytes 3145728 | tf_op jit(solution)/shard_map/all_to_all | solution.py:809
  17.3 4.0 %prep.1 = (bf16[168,168]{1,0:T(8,128)(2,1)}, bf16[80,256]{1,0:T(8,128)(2,1)}, bf16[280,120]{1,0:T(8,128)(2,1)}, bf16[112,448]{1,0:T(8,128)(2,1)}, bf16[4,160,256...) custom-call(f32[3,20,20]{2,1,0:T(8,128)} %stiff_ref.1, ...), custom_call_target="tpu_custom_call" | custom-call | tf_op jit(solution)/shard_map/prep/pallas_call | solution.py:269
  21.3 19.0 %main.1 = (f32[280,2048]{1,0:T(8,128)}, f32[280,2048]{1,0:T(8,128)}, f32[280,256]{1,0:T(8,128)}, f32[280,256]{1,0:T(8,128)}, s32[4,2048]{1,0:T(4,128)}) custom-call(f32[13,20,2048]{2,1,0:T(8,128)} %coef_ref.3, f32[3,3,2048]{2,1,0:T(4,128)} %geo_ref.3, f32[4,2048]{1,0:T(4,128)} %scale_ref.5, s32[4,2048]{1,0:T(4,128)} %beside_ref.1, ...), custom_call_target="tpu_custom_call" | custom-call | tf_op jit(solution)/shard_map/main/pallas_call | solution.py:463
  40.3 1.8 %all-to-all-done.arr_ref = f32[128,8,384]{2,1,0:T(8,128)S(1)} async-done(((f32[128,8,384]{2,1,0:T(8,128)}), f32[128,8,384]{2,1,0:T(8,128)S(1)}, u32[]{:S(2)}, u32[]{:S(2)}) %all-to-all-start) | async-done | bytes 1572896 | tf_op jit(solution)/shard_map/all_to_all | solution.py:809
  42.2 0.0 copy-start
  42.2 3.0 %collective-permute-start = (f32[280,256]{1,0:T(8,128)}, f32[280,256]{1,0:T(8,128)S(1)}, u32[]{:S(2)}, u32[]{:S(2)}) collective-permute-start(f32[280,256]{1,0:T(8,128)} %get-tuple-element.39), channel_id=1, source_target_pairs={{0,1},{1,2},{2,3},{3,4},{4,5},{5,6},{6,7},{7,8},{8,9},{9,10},{10,1... | collective-permute-start | bytes 860168 | tf_op jit(solution)/shard_map/ppermute | solution.py:830
  45.2 2.1 %collective-permute-start.1 = (f32[280,256]{1,0:T(8,128)}, f32[280,256]{1,0:T(8,128)S(1)}, u32[]{:S(2)}, u32[]{:S(2)}) collective-permute-start(f32[280,256]{1,0:T(8,128)} %get-tuple-element.40), channel_id=1, source_target_pairs={{1,0},{2,1},{3,2},{4,3},{5,4},{6,5},{7,6},{8,7},{9,8},{10,9},{11,1... | collective-permute-start | bytes 860168 | tf_op jit(solution)/shard_map/ppermute | solution.py:831
  47.3 0.0 copy-done
  47.3 13.1 %fault.1 = (f32[1024,128]{1,0:T(8,128)}, f32[16,256]{1,0:T(8,128)}, f32[16,256]{1,0:T(8,128)}) custom-call(s32[256]{0:T(256)} %minus_ref.1, s32[256]{0:T(256)} %plus_ref.1, f32[128,8,384]{2,1,0:T(8,128)} %copy-done, bf16[504,168]{1,0:T(8,128)(2,1)} %get-tuple-element.35.jq_ref, bf16[120,384]{1,0:T(8,128)(2,1)} %get-tuple-element.36.sp_ref, ...), custom_call_target="tpu_custom_call" | custom-call | tf_op jit(solution)/shard_map/fault/pallas_call | solution.py:633
  60.4 0.0 collective-permute-done.low_ref
  60.4 0.0 copy-start.2
  60.4 0.0 collective-permute-done.1.high_ref
  60.4 0.0 copy-start.3
  60.4 8.6 %all-to-all-start.1 = ((f32[128,8,128]{2,1,0:T(8,128)}), f32[128,8,128]{2,1,0:T(8,128)S(1)}, u32[]{:S(2)}, u32[]{:S(2)}) async-start(f32[128,8,128]{2,1,0:T(8,128)} %bitcast.10), calls=%async_computation.1 | async-start | bytes 1048576 | tf_op jit(solution)/shard_map/all_to_all | solution.py:849
  69.0 0.0 copy-done.2
  69.1 0.0 copy-done.3
  69.1 15.5 %beside.1.part_ref = f32[280,2048]{1,0:T(8,128)} custom-call(s32[4,2048]{1,0:T(4,128)} %get-tuple-element.42.index_ref, f32[280,2048]{1,0:T(8,128)} %get-tuple-element.43.integ_ref, f32[280,256]{1,0:T(8,128)} %copy-done.2, f32[280,256]{1,0:T(8,128)} %copy-done.3, f32[280,2048]{1,0:T(8,128)} %get-tuple-element.46.part_ref, f32[4,2048]{1,0:T(4,128)} %scale_ref.5, ...), custom_call_target="tpu_custom_call" | custom-call | tf_op jit(solution)/shard_map/beside/pallas_call | solution.py:705
  84.5 0.0 all-to-all-done.1
  84.5 0.0 copy-start.1
  84.5 0.8 copy-done.1
  85.3 6.2 %lift.1 = f32[13,20,2048]{2,1,0:T(8,128)} custom-call(s32[8,128]{1,0:T(8,128)} %bitcast.14, f32[1024,128]{1,0:T(8,128)} %bitcast.9, f32[280,2048]{1,0:T(8,128)} %beside.1.part_ref, f32[4,2048]{1,0:T(4,128)} %scale_ref.5, bf16[560,256]{1,0:T(8,128)(2,1)} %get-tuple-element.50.lift_ref), custom_call_target="tpu_custom_call" | custom-call | tf_op jit(solution)/shard_map/lift/pallas_call | solution.py:758
Async XLA Ops:
  5.7 36.4 %all-to-all-start = ((f32[128,8,384]{2,1,0:T(8,128)}), f32[128,8,384]{2,1,0:T(8,128)S(1)}, u32[]{:S(2)}, u32[]{:S(2)}) async-start(f32[128,8,384]{2,1,0:T(8,128)} %send.1), calls=%async_computation | async-start | bytes 3145728 | tf_op jit(solution)/shard_map/all_to_all | solution.py:809
  42.2 5.2 %copy-start = (f32[128,8,384]{2,1,0:T(8,128)}, f32[128,8,384]{2,1,0:T(8,128)S(1)}, u32[]{:S(2)}) copy-start(f32[128,8,384]{2,1,0:T(8,128)S(1)} %all-to-all-done.arr_ref) | copy-start | bytes 4718596
  42.2 18.2 %collective-permute-start = (f32[280,256]{1,0:T(8,128)}, f32[280,256]{1,0:T(8,128)S(1)}, u32[]{:S(2)}, u32[]{:S(2)}) collective-permute-start(f32[280,256]{1,0:T(8,128)} %get-tuple-element.39), channel_id=1, source_target_pairs={{0,1},{1,2},{2,3},{3,4},{4,5},{5,6},{6,7},{7,8},{8,9},{9,10},{10,1... | collective-permute-start | bytes 860168 | tf_op jit(solution)/shard_map/ppermute | solution.py:830
  45.2 15.2 %collective-permute-start.1 = (f32[280,256]{1,0:T(8,128)}, f32[280,256]{1,0:T(8,128)S(1)}, u32[]{:S(2)}, u32[]{:S(2)}) collective-permute-start(f32[280,256]{1,0:T(8,128)} %get-tuple-element.40), channel_id=1, source_target_pairs={{1,0},{2,1},{3,2},{4,3},{5,4},{6,5},{7,6},{8,7},{9,8},{10,9},{11,1... | collective-permute-start | bytes 860168 | tf_op jit(solution)/shard_map/ppermute | solution.py:831
  60.4 8.7 %copy-start.2 = (f32[280,256]{1,0:T(8,128)}, f32[280,256]{1,0:T(8,128)S(1)}, u32[]{:S(2)}) copy-start(f32[280,256]{1,0:T(8,128)S(1)} %collective-permute-done.low_ref) | copy-start | bytes 860164
  60.4 8.6 %copy-start.3 = (f32[280,256]{1,0:T(8,128)}, f32[280,256]{1,0:T(8,128)S(1)}, u32[]{:S(2)}) copy-start(f32[280,256]{1,0:T(8,128)S(1)} %collective-permute-done.1.high_ref) | copy-start | bytes 860164
  60.4 24.1 %all-to-all-start.1 = ((f32[128,8,128]{2,1,0:T(8,128)}), f32[128,8,128]{2,1,0:T(8,128)S(1)}, u32[]{:S(2)}, u32[]{:S(2)}) async-start(f32[128,8,128]{2,1,0:T(8,128)} %bitcast.10), calls=%async_computation.1 | async-start | bytes 1048576 | tf_op jit(solution)/shard_map/all_to_all | solution.py:849
  84.5 0.8 copy-start.1
